TPU v7x, 32 devices: a whole 2x2x4 slice. The times are simulated.
32 devices in a mesh: grp: 2 (over y), gy: 4 (over z), gz: 2 (over x), vert: 2 (over core).
Axes of the slice: x: 2, y: 2, z: 4, core: 2. Of those that a mesh axis runs over, the one named last changes fastest.
Arguments:
- field: float32 [16, 64, 64, 512], P(('grp', 'vert'), 'gy', 'gz'), parts along dimension 0, as said below
- omega_x: float32 [512, 128], replicated, may hold values from -6 to 6
- omega_y: float32 [64, 32], replicated, may hold values from -6 to 6
- rank_x: int32 [2], P('grp'), parts along dimension 0, may hold values from 64 to 128
- rank_y: int32 [2], P('grp'), parts along dimension 0, may hold values from 16 to 32
Outputs:
- core: float32 [16, 32, 64, 128], P(('grp', 'vert'), 'gy', 'gz'), parts along dimension 0
- factor_x: float32 [1024, 128], P('grp'), parts along dimension 0
- factor_y: float32 [128, 32], P('grp'), parts along dimension 0
There are 2 independent parts, one for each index of `grp`. A program takes and returns all parts, laid end to end along the dimension named above; an argument that names none is the same for every part. Nothing has to cross between parts.
Inputs may be any that keep to these rules, and one draw needn't show every extreme that they name: field values are finite and of order one; their spread differs between cells of the first dimension.
All inputs are finite; a program needn't handle non-finite values.
Results may differ from a plain program's by a relative error of at most 0.000086.
Values sent between devices are 32-bit elements; how exact they have to be, the bound alone decides.
A program may use at most 64 MiB of HBM per device.

v0:
```python
import jax
import jax.numpy as jnp
from jax import lax
from jax.sharding import PartitionSpec as P


def orthonormal(sketch, trunc_rank):
    precise = lax.Precision.HIGHEST
    small_gram = jnp.dot(sketch.T, sketch, precision=precise)
    lower_factor = jnp.linalg.cholesky(small_gram)
    basis = lax.linalg.triangular_solve(
        lower_factor, sketch, left_side=False, lower=True, transpose_a=True
    )
    column_ids = jnp.arange(sketch.shape[1], dtype=jnp.int32)
    kept = (column_ids < trunc_rank[0]).astype(jnp.float32)
    return basis * kept[None, :]


def body(field, omega_x, omega_y, rank_x, rank_y):
    precise = lax.Precision.HIGHEST
    planes, rows_y, rows_z, cells_x = field.shape
    all_planes = planes * lax.axis_size("vert")
    all_rows_y = rows_y * lax.axis_size("gy")
    all_rows_z = rows_z * lax.axis_size("gz")
    flat = field.reshape(-1, cells_x)
    local_gram = jnp.dot(flat.T, flat, precision=precise)
    gram_x = lax.psum(local_gram, ("gy", "gz", "vert")) / float(
        all_planes * all_rows_y * all_rows_z
    )
    sketch_x = jnp.dot(gram_x, omega_x, precision=precise)
    factor_x = orthonormal(sketch_x, rank_x)
    ranks_x = factor_x.shape[1]
    core_x = jnp.dot(flat, factor_x, precision=precise).reshape(planes, rows_y, rows_z, ranks_x)
    spread = lax.all_to_all(core_x, "gy", split_axis=2, concat_axis=1, tiled=True)
    divisor_y = float(all_planes * all_rows_z * ranks_x)
    local_gram_y = jnp.einsum("vazr,vbzr->ab", spread, spread, precision=precise)
    gram_y = lax.psum(local_gram_y, ("gy", "gz", "vert")) / divisor_y
    sketch_y = jnp.dot(gram_y, omega_y, precision=precise)
    factor_y = orthonormal(sketch_y, rank_y)
    own_rows = lax.dynamic_slice_in_dim(factor_y, lax.axis_index("gy") * rows_y, rows_y, 0)
    partial_core = jnp.einsum("vyzr,yk->vkzr", core_x, own_rows, precision=precise)
    core = lax.psum_scatter(partial_core, "gy", scatter_dimension=1, tiled=True)
    return (core, factor_x, factor_y)


def solution(mesh):
    in_specs = (P(("grp", "vert"), "gy", "gz", None), P(), P(), P("grp"), P("grp"))
    out_specs = (P(("grp", "vert"), "gy", "gz", None), P("grp", None), P("grp", None))
    return jax.shard_map(body, mesh=mesh, in_specs=in_specs, out_specs=out_specs, check_vma=False)
```

profile of v0, /device:TPU:0, one launch (start us, length us, event | category | flops | bytes accessed | tf_op | source)
XLA Modules:
  0.0 297.8 jit_solution(9026091987991495649)
XLA Ops:
  7.2 0.0 all-reduce.2.cloned.1.call-start
  7.2 10.3 %convolution_bitcast_fusion.2 = f32[512,512]{1,0:T(8,128)} fusion(f32[4,16,32,512]{3,2,1,0:T(8,128)} %param.5), kind=kOutput, calls=%fused_computation.2 | convolution fusion | flops 6442450944 | bytes 5242880 | tf_op jit(solution)/shard_map/dot_general | solution.py:26
  17.5 0.0 all-reduce.2.cloned.1.call-update
  18.2 95.4 %all-reduce.2.cloned.1.call-done = f32[512,512]{1,0:T(8,128)} async-done(((f32[512,512]{1,0:T(8,128)}), f32[512,512]{1,0:T(8,128)}) %all-reduce.2.cloned.1.call-update) | async-done | bytes 1048592 | tf_op jit(solution)/shard_map/psum | solution.py:27
  113.7 2.2 fusion.2
  115.9 0.6 fusion.19
  116.5 0.1 copy.20
  116.6 11.7 %cholesky.29 = f32[128,128]{1,0:T(8,128)S(1)} custom-call(f32[128,128]{1,0:T(8,128)S(1)} %fusion.7), custom_call_target="Cholesky" | custom-call | tf_op jit(solution)/shard_map/jit(cholesky)/cholesky | solution.py:10
  128.3 0.6 compare_reduce_fusion.1
  129.0 0.7 fusion.5
  129.6 9.8 %custom-call.12 = f32[1,128,128]{1,2,0:T(8,128)S(1)} custom-call(f32[1,128,128]{2,1,0:T(8,128)S(1)} %fusion.5), custom_call_target="InvertDiagBlocksLowerTriangular" | custom-call | tf_op jit(solution)/shard_map/triangular_solve | solution.py:11
  139.5 0.4 convolution_multiply_fusion
  139.8 6.7 %convolution_bitcast_fusion = f32[2048,128]{0,1:T(8,128)S(1)} fusion(f32[512,128]{1,0:T(8,128)S(1)} %convolution_multiply_fusion, f32[2048,512]{1,0:T(8,128)} %bitcast.57), kind=kOutput, calls=%fused_computation | convolution fusion | flops 1610612736 | bytes 5505024 | tf_op jit(solution)/shard_map/dot_general | solution.py:33
  146.6 0.3 copy.21
  146.9 1.8 copy.22
  148.8 3.8 %all-to-all-start = ((f32[4,16,32,128]{3,1,0,2:T(8,128)}), f32[4,16,32,128]{3,1,0,2:T(8,128)S(1)}, u32[]{:S(2)}, u32[]{:S(2)}) async-start(f32[4,16,32,128]{3,1,0,2:T(8,128)} %copy.22), calls=%async_computation | async-start | bytes 2097152 | tf_op jit(solution)/shard_map/all_to_all | solution.py:34
  153.2 24.4 %all-to-all-done = f32[4,16,32,128]{3,1,0,2:T(8,128)S(1)} async-done(((f32[4,16,32,128]{3,1,0,2:T(8,128)}), f32[4,16,32,128]{3,1,0,2:T(8,128)S(1)}, u32[]{:S(2)}, u32[]{:S(2)}) %all-to-all-start) | async-done | bytes 1048608 | tf_op jit(solution)/shard_map/all_to_all | solution.py:34
  177.6 0.6 copy.24
  178.3 1.0 convolution_bitcast_fusion.3
  179.2 57.6 %psum.15 = f32[64,64]{1,0:T(8,128)S(1)} all-reduce(f32[64,64]{1,0:T(8,128)S(1)} %convolution_bitcast_fusion.3), channel_id=1, replica_groups=mesh['grp'=2,'gy'=4,'gz'=2,'vert'=2] {'gy','gz','vert'}, use_global_device_ids=true, to_apply=%region_3.4 | all-reduce | flops 4096 | bytes 32768 | tf_op jit(solution)/shard_map/psum | solution.py:37
  236.9 0.2 fusion.8
  237.0 0.1 fusion.20
  237.2 0.1 copy.27
  237.3 2.9 cholesky.61
  240.2 0.6 compare_reduce_fusion
  240.9 0.7 fusion.10
  241.5 2.5 custom-call.13
  244.0 0.2 convolution_multiply_fusion.1
  244.2 3.5 %convolution_bitcast_fusion.1 = f32[4,32,32,128]{3,1,2,0:T(8,128)} fusion(f32[4,16,32,128]{3,2,1,0:T(8,128)S(1)} %bitcast.56, f32[64,32]{0,1:T(8,128)S(1)} %convolution_multiply_fusion.1, s32[]{:T(128)S(6)} %select_n.13), kind=kOutput, calls=%fused_computation.1 | convolution fusion | flops 100663296 | bytes 3153924 | tf_op jit(solution)/shard_map/vyzr,yk->vkzr/dot_general | solution.py:41
  247.8 0.0 reduce-scatter.2.cloned.1.call-update
  247.8 41.3 %reduce-scatter.2.cloned.1.call-done = f32[4,8,32,128]{3,1,2,0:T(8,128)} async-done(((f32[4,32,32,128]{3,1,2,0:T(8,128)}), f32[4,8,32,128]{3,1,2,0:T(8,128)}) %reduce-scatter.2.cloned.1.call-update) | async-done | bytes 524304 | tf_op jit(solution)/shard_map/reduce_scatter | solution.py:42
  289.1 1.9 copy.30
  (15 shorter events, 0.1 us)
Async XLA Ops:
  7.2 106.5 %copy-start = (f32[512,128]{1,0:T(8,128)S(1)}, f32[512,128]{1,0:T(8,128)}, u32[]{:S(2)}) copy-start(f32[512,128]{1,0:T(8,128)} %param.6) | copy-start | bytes 786436
  7.2 106.5 %all-reduce.2.cloned.1.call-start = ((), (), s32[]{:S(2)}) async-start(), calls=%async_computation.2 | async-start | bytes 2097152 | tf_op jit(solution)/shard_map/psum | solution.py:27
  139.8 8.9 %copy-start.1 = (f32[512,128]{1,0:T(8,128)}, f32[512,128]{1,0:T(8,128)S(1)}, u32[]{:S(2)}) copy-start(f32[512,128]{1,0:T(8,128)S(1)} %convolution_multiply_fusion) | copy-start | bytes 786436
  146.9 89.9 %copy-start.3 = (f32[64,32]{0,1:T(8,128)S(1)}, f32[64,32]{0,1:T(8,128)}, u32[]{:S(2)}) copy-start(f32[64,32]{0,1:T(8,128)} %param.7) | copy-start | bytes 24580
  148.8 28.9 %all-to-all-start = ((f32[4,16,32,128]{3,1,0,2:T(8,128)}), f32[4,16,32,128]{3,1,0,2:T(8,128)S(1)}, u32[]{:S(2)}, u32[]{:S(2)}) async-start(f32[4,16,32,128]{3,1,0,2:T(8,128)} %copy.22), calls=%async_computation | async-start | bytes 2097152 | tf_op jit(solution)/shard_map/all_to_all | solution.py:34
  152.6 136.5 %reduce-scatter.2.cloned.1.call-start = ((), (), s32[]{:S(2)}) async-start(), calls=%async_computation.3 | async-start | bytes 2621440 | tf_op jit(solution)/shard_map/reduce_scatter | solution.py:42
  244.2 46.8 %copy-start.2 = (f32[64,32]{0,1:T(8,128)}, f32[64,32]{0,1:T(8,128)S(1)}, u32[]{:S(2)}) copy-start(f32[64,32]{0,1:T(8,128)S(1)} %convolution_multiply_fusion.1) | copy-start | bytes 24580
Sparse Core Ops, SparseCore 0:
  17.7 95.9 all-reduce.1
  247.9 41.0 reduce-scatter.1
where the time goes:
time: 298 us
  waiting for transfers between devices  161 us (54%)
  blocking collectives  57.6 us (19%)
  other arithmetic  29.6 us (10%)
  matrix products  25.3 us (8%)
  between operations  15.5 us (5%)
  local copies, waits for them, and re-layouts  4.87 us (2%)
  starting transfers between devices  3.84 us (1%)
    psum x1, waiting for transfers between devices, body(): lax.psum(local_gram, ('gy', 'gz', 'vert'))  95.4 us
    psum x1, blocking collectives, body(): gram_y = lax.psum(local_gram_y, ('gy', 'gz', 'vert')) / divisor_y  57.6 us
    reduce_scatter x1, waiting for transfers between devices, body(): core = lax.psum_scatter(partial_core, 'gy', scatter_dimension=1, tiled=True)  41.3 us
    all_to_all x1, waiting for transfers between devices, body(): lax.all_to_all(core_x, 'gy', split_axis=2, concat_axis=1, tiled=True)  24.4 us
    another operation x6, other arithmetic, orthonormal(): lower_factor = jnp.linalg.cholesky(small_gram)  16 us
    another operation x4, other arithmetic, orthonormal(): lax.linalg.triangular_solve(lower_factor, sketch, left_side=False, lower=...  13.6 us
    dot_general x1, matrix products, body(): local_gram = jnp.dot(flat.T, flat, precision=precise)  10.3 us
    dot_general x1, matrix products, body(): jnp.dot(flat, factor_x, precision=precise)  6.75 us
  transfers between devices with their start and end apart: 3, of which 3 were waited for; matrix products, arithmetic and copies ran while one was open for 0% of the time, Pallas kernels for 0%

commit v1 on v0

v1 whole, which is shorter than its diff:
```python
import jax
import jax.numpy as jnp
from jax import lax
from jax.sharding import PartitionSpec as P

HIGHEST = lax.Precision.HIGHEST


def inverse_factor(sketch):
    small_gram = jnp.dot(sketch.T, sketch, precision=HIGHEST)
    lower = jnp.linalg.cholesky(small_gram)
    eye = jnp.eye(lower.shape[0], dtype=jnp.float32)
    return lax.linalg.triangular_solve(lower, eye, left_side=True, lower=True)


def plain_body(field, omega_x, omega_y, rank_x, rank_y):
    planes, rows_y, rows_z, cells_x = field.shape
    all_planes = planes * lax.axis_size("vert")
    all_rows_y = rows_y * lax.axis_size("gy")
    all_rows_z = rows_z * lax.axis_size("gz")
    flat = field.reshape(-1, cells_x)
    proj = jnp.dot(flat, omega_x, precision=HIGHEST)
    local_sketch = jnp.dot(flat.T, proj, precision=HIGHEST)
    sketch_x = lax.psum(local_sketch, ("gy", "gz", "vert")) / float(all_planes * all_rows_y * all_rows_z)
    ranks_x = sketch_x.shape[1]
    terms = jnp.dot(flat, sketch_x, precision=HIGHEST).reshape(planes, rows_y, rows_z, ranks_x)
    spread = lax.all_to_all(terms, "gy", split_axis=2, concat_axis=1, tiled=True)
    inv_x = inverse_factor(sketch_x)
    kept_x = (jnp.arange(ranks_x) < rank_x[0]).astype(jnp.float32)
    inv_x = inv_x * kept_x[:, None]
    factor_x = jnp.dot(sketch_x, inv_x.T, precision=HIGHEST)
    core_x = jnp.einsum("vyzr,sr->vyzs", spread, inv_x, precision=HIGHEST)
    divisor_y = float(all_planes * all_rows_z * ranks_x)
    local_gram_y = jnp.einsum("vazr,vbzr->ab", core_x, core_x, precision=HIGHEST)
    sketch_y = lax.psum(jnp.dot(local_gram_y, omega_y, precision=HIGHEST), ("gy", "gz", "vert")) / divisor_y
    inv_y = inverse_factor(sketch_y)
    kept_y = (jnp.arange(inv_y.shape[0]) < rank_y[0]).astype(jnp.float32)
    factor_y = jnp.dot(sketch_y, (inv_y * kept_y[:, None]).T, precision=HIGHEST)
    mine = jnp.einsum("vyzr,yk->vkzr", core_x, factor_y, precision=HIGHEST)
    core = lax.all_to_all(mine, "gy", split_axis=1, concat_axis=2, tiled=True)
    return (core, factor_x, factor_y)


def solution(mesh):
    in_specs = (P(("grp", "vert"), "gy", "gz", None), P(), P(), P("grp"), P("grp"))
    out_specs = (P(("grp", "vert"), "gy", "gz", None), P("grp", None), P("grp", None))
    return jax.shard_map(plain_body, mesh=mesh, in_specs=in_specs, out_specs=out_specs, check_vma=False)
```

time: 298 us -> 241 us (0.81)
  waiting for transfers between devices: 161 us -> 101 us
  starting transfers between devices: 3.84 us -> 8.55 us
  matrix products: 25.3 us -> 20.8 us
    reduce_scatter x1 -> x0, waiting for transfers between devices: 41.3 us -> none  [body(): core = lax.psum_scatter(partial_core, 'gy', scatter_dimension=1, tiled=True)]
    all_to_all x1 -> x2, waiting for transfers between devices: 24.4 us -> 9.27 us  [the longest x1 9.08 us: plain_body(): core = lax.all_to_all(mine, 'gy', split_axis=1, concat_axis=2, tiled=True)]
    all_to_all x1 -> x2, starting transfers between devices: 3.8 us -> 8.51 us  [the longest x1 5.04 us: plain_body(): lax.all_to_all(terms, 'gy', split_axis=2, concat_axis=1, tiled=True)]
    dot_general x8 -> x11, matrix products: 24.7 us -> 20.4 us  [the longest x1 6.59 us: plain_body(): jnp.dot(flat, sketch_x, precision=HIGHEST)]
    psum x1, waiting for transfers between devices: 95.4 us -> 91.6 us  [plain_body(): lax.psum(local_sketch, ('gy', 'gz', 'vert'))]
  transfers between devices with their start and end apart: 3 -> 3, of which waited for: 3 -> 3; matrix products, arithmetic and copies ran while one was open for 0% -> 10% of each run, Pallas kernels for 0% -> 0%
where the time goes in v1:
time: 241 us; the launch traced here: 240 us
  waiting for transfers between devices  101 us (42%)
  blocking collectives  59.5 us (25%)
  other arithmetic  29.6 us (12%)
  matrix products  20.8 us (9%)
  between operations  15.5 us (6%)
  starting transfers between devices  8.55 us (4%)
  local copies, waits for them, and re-layouts  5.58 us (2%)
    psum x1, waiting for transfers between devices, plain_body(): lax.psum(local_sketch, ('gy', 'gz', 'vert'))  91.6 us
    psum x1, blocking collectives, plain_body(): lax.psum(jnp.dot(local_gram_y, omega_y, precision=HIGHEST), ('gy', 'gz',...  59.5 us
    another operation x6, other arithmetic, inverse_factor(): lower = jnp.linalg.cholesky(small_gram)  16 us
    another operation x4, other arithmetic, inverse_factor(): return lax.linalg.triangular_solve(lower, eye, left_side=True, lower=True)  13.6 us
    all_to_all x1, waiting for transfers between devices, plain_body(): core = lax.all_to_all(mine, 'gy', split_axis=1, concat_axis=2, tiled=True)  9.08 us
    dot_general x1, matrix products, plain_body(): jnp.dot(flat, sketch_x, precision=HIGHEST)  6.59 us
    dot_general x1, matrix products, plain_body(): proj = jnp.dot(flat, omega_x, precision=HIGHEST)  5.6 us
    all_to_all x1, starting transfers between devices, plain_body(): lax.all_to_all(terms, 'gy', split_axis=2, concat_axis=1, tiled=True)  5.04 us
  transfers between devices with their start and end apart: 3, of which 3 were waited for; matrix products, arithmetic and copies ran while one was open for 10% of the time, Pallas kernels for 0%

profile of v1, /device:TPU:0, one launch (start us, length us, event | category | flops | bytes accessed | tf_op | source)
XLA Modules:
  0.0 240.5 jit_solution(7376903615995343693)
XLA Ops:
  7.2 0.9 copy-done
  8.1 5.6 %fusion.29 = f32[2048,128]{1,0:T(8,128)S(1)} fusion(f32[2048,512]{1,0:T(8,128)} %bitcast.66, f32[512,128]{1,0:T(8,128)S(1)} %copy-done), kind=kOutput, calls=%fused_computation.50 | convolution fusion | flops 1610612736 | bytes 5505024 | tf_op jit(solution)/shard_map/dot_general | solution.py:22
  13.7 3.5 %convolution_bitcast_fusion.2 = f32[512,128]{0,1:T(8,128)} fusion(f32[2048,128]{1,0:T(8,128)S(1)} %fusion.29, f32[2048,512]{1,0:T(8,128)S(1)} %bitcast.68), kind=kOutput, calls=%fused_computation.2 | convolution fusion | flops 1610612736 | bytes 5505024 | tf_op jit(solution)/shard_map/dot_general | solution.py:23
  17.2 91.6 %all-reduce.2.cloned.1.call-done = f32[512,128]{0,1:T(8,128)} async-done(((f32[512,128]{0,1:T(8,128)}), f32[512,128]{0,1:T(8,128)}) %all-reduce.2.cloned.1.call-update) | async-done | bytes 262160 | tf_op jit(solution)/shard_map/psum | solution.py:24
  108.9 6.6 %convolution_bitcast_fusion = f32[2048,128]{0,1:T(8,128)S(1)} fusion(f32[2048,512]{1,0:T(8,128)} %bitcast.67, f32[512,128]{0,1:T(8,128)} %all-reduce.2.cloned.1.call-done), kind=kOutput, calls=%fused_computation | convolution fusion | flops 1610678272 | bytes 5505024 | tf_op jit(solution)/shard_map/dot_general | solution.py:26
  115.5 0.3 copy.19
  115.8 1.6 copy.20
  117.4 5.0 %all-to-all-start = ((f32[4,16,32,128]{3,1,0,2:T(8,128)}), f32[4,16,32,128]{3,1,0,2:T(8,128)S(1)}, u32[]{:S(2)}, u32[]{:S(2)}) async-start(f32[4,16,32,128]{3,1,0,2:T(8,128)} %copy.20), calls=%async_computation | async-start | bytes 2097152 | tf_op jit(solution)/shard_map/all_to_all | solution.py:27
  123.8 0.4 fusion.4
  124.3 11.7 %cholesky.31 = f32[128,128]{1,0:T(8,128)S(1)} custom-call(f32[128,128]{1,0:T(8,128)S(1)} %fusion.13), custom_call_target="Cholesky" | custom-call | tf_op jit(solution)/shard_map/jit(cholesky)/cholesky | solution.py:11
  136.0 0.6 compare_reduce_fusion.1
  136.7 0.7 fusion.10
  137.4 9.8 %custom-call.12 = f32[1,128,128]{1,2,0:T(8,128)S(1)} custom-call(f32[1,128,128]{2,1,0:T(8,128)S(1)} %fusion.10), custom_call_target="InvertDiagBlocksLowerTriangular" | custom-call | tf_op jit(solution)/shard_map/triangular_solve | solution.py:13
  147.2 0.3 convolution_multiply_fusion
  147.4 0.2 all-to-all-done
  147.6 0.6 copy.22
  148.2 1.0 fusion
  149.2 1.0 convolution_bitcast_fusion.3
  150.2 0.2 fusion.30
  150.4 59.5 %psum.15 = f32[64,32]{0,1:T(8,128)S(1)} all-reduce(f32[64,32]{0,1:T(8,128)S(1)} %fusion.30), channel_id=1, replica_groups=mesh['grp'=2,'gy'=4,'gz'=2,'vert'=2] {'gy','gz','vert'}, use_global_device_ids=true, to_apply=%region_3.4 | all-reduce | flops 2048 | bytes 16384 | tf_op jit(solution)/shard_map/psum | solution.py:35
  210.1 2.9 %cholesky.65 = f32[32,32]{1,0:T(8,128)S(1)} custom-call(f32[32,32]{1,0:T(8,128)S(1)} %fusion.17), custom_call_target="Cholesky" | custom-call | tf_op jit(solution)/shard_map/jit(cholesky)/cholesky | solution.py:11
  213.1 0.6 compare_reduce_fusion
  213.7 0.7 fusion.14
  214.4 2.4 %custom-call.13 = f32[1,32,32]{1,2,0:T(8,128)S(1)} custom-call(f32[1,32,32]{2,1,0:T(8,128)S(1)} %fusion.14), custom_call_target="InvertDiagBlocksLowerTriangular" | custom-call | tf_op jit(solution)/shard_map/triangular_solve | solution.py:13
  216.8 0.2 convolution_multiply_fusion.1
  217.0 0.2 fusion.18
  217.2 0.6 convolution_bitcast_fusion.1
  217.8 1.1 copy.28
  218.9 3.5 %all-to-all-start.1 = ((f32[4,32,8,128]{3,2,0,1:T(8,128)}), f32[4,32,8,128]{3,2,0,1:T(8,128)S(1)}, u32[]{:S(2)}, u32[]{:S(2)}) async-start(f32[4,32,8,128]{3,2,0,1:T(8,128)} %copy.28), calls=%async_computation.1 | async-start | bytes 1048576 | tf_op jit(solution)/shard_map/all_to_all | solution.py:40
  222.4 1.3 fusion.2
  223.7 9.1 %all-to-all-done.1 = f32[4,32,8,128]{3,2,0,1:T(8,128)S(1)} async-done(((f32[4,32,8,128]{3,2,0,1:T(8,128)}), f32[4,32,8,128]{3,2,0,1:T(8,128)S(1)}, u32[]{:S(2)}, u32[]{:S(2)}) %all-to-all-start.1) | async-done | bytes 524320 | tf_op jit(solution)/shard_map/all_to_all | solution.py:40
  232.8 0.9 copy.39
  (20 shorter events, 0.5 us)
Async XLA Ops:
  7.2 1.0 copy-start
  7.2 101.7 %all-reduce.2.cloned.1.call-start = ((), (), s32[]{:S(2)}) async-start(), calls=%async_computation.2 | async-start | bytes 524288 | tf_op jit(solution)/shard_map/psum | solution.py:24
  7.2 6.5 %copy-start.1 = (f32[4,16,32,512]{3,2,1,0:T(8,128)S(1)}, f32[4,16,32,512]{3,2,1,0:T(8,128)}, u32[]{:S(2)}) copy-start(f32[4,16,32,512]{3,2,1,0:T(8,128)} %param.5) | copy-start | bytes 12582916
  115.5 8.3 %copy-start.2 = (f32[512,128]{0,1:T(8,128)S(1)}, f32[512,128]{0,1:T(8,128)}, u32[]{:S(2)}) copy-start(f32[512,128]{0,1:T(8,128)} %all-reduce.2.cloned.1.call-done) | copy-start | bytes 786436
  117.4 30.2 %all-to-all-start = ((f32[4,16,32,128]{3,1,0,2:T(8,128)}), f32[4,16,32,128]{3,1,0,2:T(8,128)S(1)}, u32[]{:S(2)}, u32[]{:S(2)}) async-start(f32[4,16,32,128]{3,1,0,2:T(8,128)} %copy.20), calls=%async_computation | async-start | bytes 2097152 | tf_op jit(solution)/shard_map/all_to_all | solution.py:27
  122.5 27.7 %copy-start.4 = (f32[64,32]{0,1:T(8,128)S(1)}, f32[64,32]{0,1:T(8,128)}, u32[]{:S(2)}) copy-start(f32[64,32]{0,1:T(8,128)} %param.7) | copy-start | bytes 24580
  217.2 16.5 %copy-start.3 = (f32[64,32]{0,1:T(8,128)}, f32[64,32]{0,1:T(8,128)S(1)}, u32[]{:S(2)}) copy-start(f32[64,32]{0,1:T(8,128)S(1)} %fusion.18) | copy-start | bytes 24580
  218.9 13.9 %all-to-all-start.1 = ((f32[4,32,8,128]{3,2,0,1:T(8,128)}), f32[4,32,8,128]{3,2,0,1:T(8,128)S(1)}, u32[]{:S(2)}, u32[]{:S(2)}) async-start(f32[4,32,8,128]{3,2,0,1:T(8,128)} %copy.28), calls=%async_computation.1 | async-start | bytes 1048576 | tf_op jit(solution)/shard_map/all_to_all | solution.py:40
Sparse Core Ops, SparseCore 0:
  17.4 91.4 all-reduce.1

commit v2 on v1

--- a/solution.py
+++ b/solution.py
@@ -1,6 +1,10 @@
+import functools
+
 import jax
 import jax.numpy as jnp
 from jax import lax
+from jax.experimental import pallas as pl
+from jax.experimental.pallas import tpu as pltpu
 from jax.sharding import PartitionSpec as P
 
 HIGHEST = lax.Precision.HIGHEST
@@ -41,7 +45,253 @@
     return (core, factor_x, factor_y)
 
 
+MESH = pl.DeviceIdType.MESH
+NT = (((1,), (1,)), ((), ()))
+
+
+def mm(a, b):
+    return jnp.dot(a, b, precision=HIGHEST, preferred_element_type=jnp.float32)
+
+
+def mm_nt(a, b):
+    return lax.dot_general(a, b, NT, precision=HIGHEST, preferred_element_type=jnp.float32)
+
+
+def eliminate(work, inv, size):
+    rows = lax.broadcasted_iota(jnp.int32, (size, size), 0)
+    cols = lax.broadcasted_iota(jnp.int32, (size, size), 1)
+    inv[...] = (rows == cols).astype(jnp.float32)
+    row_ids = lax.broadcasted_iota(jnp.int32, (size, 1), 0)
+    lane_ids = lax.broadcasted_iota(jnp.int32, (1, size), 1)
+
+    def step(j, pivots):
+        full = work[...]
+        row = work[pl.ds(j, 1), :]
+        column = jnp.sum(jnp.where(cols == j, full, 0.0), axis=1, keepdims=True)
+        pivot = jnp.sum(jnp.where(lane_ids == j, row, 0.0), axis=1, keepdims=True)
+        factor = jnp.where(row_ids > j, column / pivot, 0.0)
+        inv_row = inv[pl.ds(j, 1), :]
+        work[...] = full - factor * row
+        inv[...] = inv[...] - factor * inv_row
+        return jnp.where(row_ids == j, pivot, pivots)
+
+    pivots = lax.fori_loop(0, size, step, jnp.ones((size, 1), jnp.float32))
+    inv[...] = inv[...] * lax.rsqrt(pivots)
+
+
+def fused(dims, rank_x, rank_y, field, omega_x, omega_y_t, core_out, fx_out, fy_out,
+          part, gathered, own_sum, sketch, tmp, terms, spread, slabs, back,
+          work_x, inv_x, work_y, inv_y, y_own, y_buf, y_mid, y_buf2,
+          rs_send, rs_recv, ag_send, ag_recv, t_send, t_recv,
+          y_send, y_recv, y2_send, y2_recv, b_send, b_recv):
+    ny, nz, nv, planes, rows_y, rows_z, cells, ranks_x, ranks_y, divisor_x, divisor_y = dims
+    members = ny * nz * nv
+    inner = nz * nv
+    grp = lax.axis_index("grp")
+    my_y, my_z, my_v = lax.axis_index("gy"), lax.axis_index("gz"), lax.axis_index("vert")
+    my_in = my_z * nv + my_v
+    me = my_y * inner + my_in
+
+    def device(y, i):
+        return (grp, y, i // nv, lax.rem(i, nv))
+
+    def member(m):
+        return device(m // inner, lax.rem(m, inner))
+
+    others = [lax.rem(me + k, members) for k in range(1, members)]
+    others_y = [lax.rem(my_y + k, ny) for k in range(1, ny)]
+    others_in = [lax.rem(my_in + k, inner) for k in range(1, inner)]
+
+    barrier = pltpu.get_barrier_semaphore()
+    for m in others:
+        pl.semaphore_signal(barrier, inc=1, device_id=member(m), device_id_type=MESH)
+
+    part[...] = jnp.zeros_like(part)
+    omega = omega_x[...]
+    chunk = 256
+    per_plane = rows_y * rows_z // chunk
+
+    def sketch_step(c, carry):
+        block = field[pl.ds(pl.multiple_of(c * chunk, chunk), chunk), :]
+        proj = mm(block, omega)
+        part[...] += mm(proj.T, block)
+        return carry
+
+    lax.fori_loop(0, planes * per_plane, sketch_step, 0)
+    pl.semaphore_wait(barrier, members - 1)
+
+    def remote(src, dst, send, recv, target):
+        return pltpu.make_async_remote_copy(src_ref=src, dst_ref=dst, send_sem=send, recv_sem=recv,
+                                            device_id=target, device_id_type=MESH)
+
+    share = ranks_x // members
+
+    def part_rows(m):
+        return pl.ds(pl.multiple_of(m * share, share), share)
+
+    def rs_copy(m, slot):
+        return remote(part.at[part_rows(m)], gathered.at[slot], rs_send.at[m], rs_recv.at[slot], member(m))
+
+    for m in others:
+        rs_copy(m, me).start()
+    gathered[me] = part[part_rows(me), :]
+    for m in others:
+        rs_copy(m, m).wait_recv()
+    total = gathered[0]
+    for m in range(1, members):
+        total = total + gathered[m]
+    total = total / divisor_x
+    own_sum[...] = total
+    sketch[part_rows(me), :] = total
+
+    def ag_copy(m, slot):
+        return remote(own_sum, sketch.at[part_rows(slot)], ag_send.at[m], ag_recv.at[slot], member(m))
+
+    for m in others:
+        ag_copy(m, me).start()
+    for m in others:
+        ag_copy(m, m).wait_recv()
+
+    depth = rows_z // ny
+    sketch_t = sketch[...]
+
+    def t_copy(v, y, slot):
+        return remote(terms.at[v, pl.ds(pl.multiple_of(y * depth, depth), depth)],
+                      spread.at[v, :, pl.ds(pl.multiple_of(slot * rows_y, rows_y), rows_y)],
+                      t_send.at[v, y], t_recv.at[v, slot], device(y, my_in))
+
+    for v in range(planes):
+        for c in range(per_plane):
+            start = (v * per_plane + c) * chunk
+            tmp[pl.ds(c * chunk, chunk), :] = mm_nt(field[pl.ds(start, chunk), :], sketch_t)
+        for z in range(rows_z):
+            terms[v, z] = tmp[pl.ds(z, rows_y, stride=rows_z), :]
+        for y in others_y:
+            t_copy(v, y, my_y).start()
+        spread[v, :, pl.ds(pl.multiple_of(my_y * rows_y, rows_y), rows_y), :] = (
+            terms[v, pl.ds(pl.multiple_of(my_y * depth, depth), depth)])
+
+    work_x[...] = mm_nt(sketch_t, sketch_t)
+    eliminate(work_x, inv_x, ranks_x)
+    kept_x = lax.broadcasted_iota(jnp.int32, (ranks_x, 1), 0) < rank_x[0]
+    right = jnp.where(kept_x, inv_x[...], 0.0)
+    fx_out[...] = mm(right, sketch_t).T
+
+    all_y = ny * rows_y
+    for v in range(planes):
+        for y in others_y:
+            t_copy(v, y, y).wait_recv()
+        block = mm_nt(spread[v].reshape(depth * all_y, ranks_x), right)
+        for z in range(depth):
+            slabs[:, pl.ds((v * depth + z) * ranks_x, ranks_x)] = block[z * all_y:(z + 1) * all_y, :]
+    gram = mm_nt(slabs[...], slabs[...])
+    y_own[...] = mm(omega_y_t[...], gram)
+
+    def y_copy(i, slot):
+        return remote(y_own, y_buf.at[slot], y_send.at[i], y_recv.at[slot], device(my_y, i))
+
+    for i in others_in:
+        y_copy(i, my_in).start()
+    y_buf[my_in] = y_own[...]
+    for i in others_in:
+        y_copy(i, i).wait_recv()
+    total = y_buf[0]
+    for i in range(1, inner):
+        total = total + y_buf[i]
+    y_mid[...] = total
+
+    def y2_copy(y, slot):
+        return remote(y_mid, y_buf2.at[slot], y2_send.at[y], y2_recv.at[slot], device(y, my_in))
+
+    for y in others_y:
+        y2_copy(y, my_y).start()
+    y_buf2[my_y] = total
+    for y in others_y:
+        y2_copy(y, y).wait_recv()
+    total = y_buf2[0]
+    for y in range(1, ny):
+        total = total + y_buf2[y]
+    sketch_y_t = total / divisor_y
+
+    work_y[...] = mm_nt(sketch_y_t, sketch_y_t)
+    eliminate(work_y, inv_y, ranks_y)
+    kept_y = lax.broadcasted_iota(jnp.int32, (ranks_y, 1), 0) < rank_y[0]
+    factor_y_t = mm(jnp.where(kept_y, inv_y[...], 0.0), sketch_y_t)
+    fy_out[...] = factor_y_t.T
+
+    share_k = ranks_y // ny
+
+    def b_copy(y, slot):
+        return remote(back.at[:, pl.ds(pl.multiple_of(y * share_k, share_k), share_k)],
+                      core_out.at[:, :, pl.ds(pl.multiple_of(slot * depth, depth), depth)],
+                      b_send.at[y], b_recv.at[slot], device(y, my_in))
+
+    for v in range(planes):
+        width = depth * ranks_x
+        block = mm(factor_y_t, slabs[:, pl.ds(v * width, width)])
+        for z in range(depth):
+            back[v, :, z, :] = block[:, z * ranks_x:(z + 1) * ranks_x]
+    for y in others_y:
+        b_copy(y, my_y).start()
+    core_out[:, :, pl.ds(pl.multiple_of(my_y * depth, depth), depth), :] = (
+        back[:, pl.ds(pl.multiple_of(my_y * share_k, share_k), share_k)])
+    for y in others_y:
+        b_copy(y, y).wait_recv()
+
+    for m in others:
+        rs_copy(m, me).wait_send()
+        ag_copy(m, me).wait_send()
+    for y in others_y:
+        for v in range(planes):
+            t_copy(v, y, my_y).wait_send()
+        y2_copy(y, my_y).wait_send()
+        b_copy(y, my_y).wait_send()
+    for i in others_in:
+        y_copy(i, my_in).wait_send()
+
+
+def fused_body(field, omega_x, omega_y, rank_x, rank_y):
+    planes, rows_y, rows_z, cells = field.shape
+    ny, nz, nv = lax.axis_size("gy"), lax.axis_size("gz"), lax.axis_size("vert")
+    ranks_x, ranks_y = omega_x.shape[1], omega_y.shape[1]
+    members, inner, depth, all_y = ny * nz * nv, nz * nv, rows_z // ny, rows_y * ny
+    divisor_x = float(planes * nv * all_y * rows_z * nz)
+    divisor_y = float(planes * nv * rows_z * nz * ranks_x)
+    dims = (ny, nz, nv, planes, rows_y, rows_z, cells, ranks_x, ranks_y, divisor_x, divisor_y)
+    vmem = pl.BlockSpec(memory_space=pltpu.VMEM)
+    smem = pl.BlockSpec(memory_space=pltpu.SMEM)
+    dma = pltpu.SemaphoreType.DMA
+
+    def buf(*shape):
+        return pltpu.VMEM(shape, jnp.float32)
+
+    def out(*shape):
+        return jax.ShapeDtypeStruct(shape, jnp.float32)
+
+    return pl.pallas_call(
+        functools.partial(fused, dims),
+        out_shape=(out(planes, ranks_y // ny, rows_z * 1, ranks_x), out(cells, ranks_x), out(all_y, ranks_y)),
+        in_specs=[smem, smem, vmem, vmem, vmem],
+        out_specs=(vmem, vmem, vmem),
+        scratch_shapes=[
+            buf(ranks_x, cells), buf(members, ranks_x // members, cells), buf(ranks_x // members, cells),
+            buf(ranks_x, cells), buf(rows_y * rows_z, ranks_x), buf(planes, rows_z, rows_y, ranks_x),
+            buf(planes, depth, all_y, ranks_x), buf(all_y, planes * depth * ranks_x),
+            buf(planes, ranks_y, depth, ranks_x),
+            buf(ranks_x, ranks_x), buf(ranks_x, ranks_x), buf(ranks_y, ranks_y), buf(ranks_y, ranks_y),
+            buf(ranks_y, all_y), buf(inner, ranks_y, all_y), buf(ranks_y, all_y), buf(ny, ranks_y, all_y),
+            dma((members,)), dma((members,)), dma((members,)), dma((members,)),
+            dma((planes, ny)), dma((planes, ny)),
+            dma((inner,)), dma((inner,)), dma((ny,)), dma((ny,)), dma((ny,)), dma((ny,)),
+        ],
+        compiler_params=pltpu.CompilerParams(collective_id=0, has_side_effects=True,
+                                             vmem_limit_bytes=40 * 1024 * 1024),
+    )(rank_x, rank_y, field.reshape(-1, cells), omega_x, omega_y.T)
+
+
 def solution(mesh):
     in_specs = (P(("grp", "vert"), "gy", "gz", None), P(), P(), P("grp"), P("grp"))
     out_specs = (P(("grp", "vert"), "gy", "gz", None), P("grp", None), P("grp", None))
-    return jax.shard_map(plain_body, mesh=mesh, in_specs=in_specs, out_specs=out_specs, check_vma=False)
+    members = mesh.shape["gy"] * mesh.shape["gz"] * mesh.shape["vert"]
+    body = fused_body if members <= 16 and mesh.shape["gy"] <= 4 else plain_body
+    return jax.shard_map(body, mesh=mesh, in_specs=in_specs, out_specs=out_specs, check_vma=False)

time: 241 us -> 87.2 us (0.36)
  waiting for transfers between devices: 101 us -> 0 us
  Pallas kernels: 0 us -> 79 us
  blocking collectives: 59.5 us -> 0 us
  other arithmetic: 29.6 us -> 0 us
  matrix products: 20.8 us -> 0 us
  between operations: 15.5 us -> 1.94 us
  starting transfers between devices: 8.55 us -> 0 us
    psum x1 -> x0, waiting for transfers between devices: 91.6 us -> none  [plain_body(): lax.psum(local_sketch, ('gy', 'gz', 'vert'))]
    pallas_call x0 -> x1, Pallas kernels: none -> 79 us  [fused_body(): pl.pallas_call(functools.partial(fused, dims), out_shape=(out(planes, ran...]
    psum x1 -> x0, blocking collectives: 59.5 us -> none  [plain_body(): lax.psum(jnp.dot(local_gram_y, omega_y, precision=HIGHEST), ('gy', 'gz',...]
    another operation x10 -> x0, other arithmetic: 29.5 us -> none  [the longest x6 16 us: inverse_factor(): lower = jnp.linalg.cholesky(small_gram)]
    dot_general x11 -> x0, matrix products: 20.4 us -> none  [the longest x1 6.59 us: plain_body(): jnp.dot(flat, sketch_x, precision=HIGHEST)]
    all_to_all x2 -> x0, waiting for transfers between devices: 9.27 us -> none  [the longest x1 9.08 us: plain_body(): core = lax.all_to_all(mine, 'gy', split_axis=1, concat_axis=2, tiled=True)]
    all_to_all x2 -> x0, starting transfers between devices: 8.51 us -> none  [the longest x1 5.04 us: plain_body(): lax.all_to_all(terms, 'gy', split_axis=2, concat_axis=1, tiled=True)]
    unnamed x10 -> x8, local copies, waits for them, and re-layouts: 0.92 us -> 5.34 us
  transfers between devices with their start and end apart: 3 -> 0, of which waited for: 3 -> 0; matrix products, arithmetic and copies ran while one was open for 10% -> 0% of each run, Pallas kernels for 0% -> 0%
where the time goes in v2:
time: 87.2 us; the launch traced here: 86.9 us
  Pallas kernels  79 us (91%)
  local copies, waits for them, and re-layouts  6.02 us (7%)
  between operations  1.94 us (2%)
    pallas_call x1, Pallas kernels, fused_body(): pl.pallas_call(functools.partial(fused, dims), out_shape=(out(planes, ran...  79 us
    unnamed x8, local copies, waits for them, and re-layouts  5.34 us

profile of v2, /device:TPU:0, one launch (start us, length us, event | category | flops | bytes accessed | tf_op | source)
XLA Modules:
  0.0 86.9 jit_solution(14806673525671877560)
XLA Ops:
  1.9 0.0 copy-start
  1.9 2.2 %copy-done = f32[4,16,32,512]{3,2,1,0:T(8,128)S(1)} copy-done((f32[4,16,32,512]{3,2,1,0:T(8,128)S(1)}, f32[4,16,32,512]{3,2,1,0:T(8,128)}, u32[]{:S(2)}) %copy-start) | copy-done | bytes 4194328
  4.1 0.0 copy-start.1
  4.1 0.9 %copy-done.1 = f32[512,128]{1,0:T(8,128)S(1)} copy-done((f32[512,128]{1,0:T(8,128)S(1)}, f32[512,128]{1,0:T(8,128)}, u32[]{:S(2)}) %copy-start.1) | copy-done | bytes 262168
  5.1 0.0 copy-start.2
  5.1 0.7 copy-done.2
  5.8 79.0 %shard_map.76 = (f32[4,8,32,128]{3,2,1,0:T(8,128)S(1)}, f32[512,128]{1,0:T(8,128)S(1)}, f32[64,32]{1,0:T(8,128)S(1)}) custom-call(s32[1]{0:T(128)S(6)} %copy.11.rank_x, s32[1]{0:T(128)S(6)} %copy.12.rank_y, f32[2048,512]{1,0:T(8,128)S(1)} %bitcast.2, f32[512,128]{1,0:T(8,128)S(1)} %copy-done.1, f32[32,64]{1,0:T(8,128)S(1)} %bitcast.3), custom_call_target="tpu_custom_call" | custom-call | tf_op jit(solution)/shard_map/pallas_call | solution.py:271
  84.7 0.7 copy.8
  85.4 0.8 copy.13
  86.2 0.7 copy.14
Async XLA Ops:
  1.9 2.2 %copy-start = (f32[4,16,32,512]{3,2,1,0:T(8,128)S(1)}, f32[4,16,32,512]{3,2,1,0:T(8,128)}, u32[]{:S(2)}) copy-start(f32[4,16,32,512]{3,2,1,0:T(8,128)} %param.5) | copy-start | bytes 12582916
  4.1 0.9 %copy-start.1 = (f32[512,128]{1,0:T(8,128)S(1)}, f32[512,128]{1,0:T(8,128)}, u32[]{:S(2)}) copy-start(f32[512,128]{1,0:T(8,128)} %omega_x.1) | copy-start | bytes 786436
  5.1 0.7 copy-start.2

commit v3 on v2

--- a/solution.py
+++ b/solution.py
@@ -57,6 +57,18 @@
     return lax.dot_general(a, b, NT, precision=HIGHEST, preferred_element_type=jnp.float32)
 
 
+def split(x):
+    high = x.astype(jnp.bfloat16)
+    return high, (x - high.astype(jnp.float32)).astype(jnp.bfloat16)
+
+
+def mm3(a, b, dims=(((1,), (0,)), ((), ()))):
+    def one(x, y):
+        return lax.dot_general(x, y, dims, preferred_element_type=jnp.float32)
+
+    return one(a[0], b[0]) + (one(a[0], b[1]) + one(a[1], b[0]))
+
+
 def eliminate(work, inv, size):
     rows = lax.broadcasted_iota(jnp.int32, (size, size), 0)
     cols = lax.broadcasted_iota(jnp.int32, (size, size), 1)
@@ -107,14 +119,14 @@
         pl.semaphore_signal(barrier, inc=1, device_id=member(m), device_id_type=MESH)
 
     part[...] = jnp.zeros_like(part)
-    omega = omega_x[...]
+    omega = split(omega_x[...])
     chunk = 256
     per_plane = rows_y * rows_z // chunk
 
     def sketch_step(c, carry):
-        block = field[pl.ds(pl.multiple_of(c * chunk, chunk), chunk), :]
-        proj = mm(block, omega)
-        part[...] += mm(proj.T, block)
+        block = split(field[pl.ds(pl.multiple_of(c * chunk, chunk), chunk), :])
+        proj = mm3(block, omega)
+        part[...] += mm3(split(proj.T), block)
         return carry
 
     lax.fori_loop(0, planes * per_plane, sketch_step, 0)
@@ -154,6 +166,7 @@
 
     depth = rows_z // ny
     sketch_t = sketch[...]
+    sketch_parts = split(sketch_t)
 
     def t_copy(v, y, slot):
         return remote(terms.at[v, pl.ds(pl.multiple_of(y * depth, depth), depth)],
@@ -163,7 +176,7 @@
     for v in range(planes):
         for c in range(per_plane):
             start = (v * per_plane + c) * chunk
-            tmp[pl.ds(c * chunk, chunk), :] = mm_nt(field[pl.ds(start, chunk), :], sketch_t)
+            tmp[pl.ds(c * chunk, chunk), :] = mm3(split(field[pl.ds(start, chunk), :]), sketch_parts, NT)
         for z in range(rows_z):
             terms[v, z] = tmp[pl.ds(z, rows_y, stride=rows_z), :]
         for y in others_y:

time: 87.2 us -> 81.4 us (0.933)
  Pallas kernels: 79 us -> 73.1 us
    pallas_call x1, Pallas kernels: 79 us -> 73.1 us  [fused_body(): pl.pallas_call(functools.partial(fused, dims), out_shape=(out(planes, ran...]
where the time goes in v3:
time: 81.4 us; the launch traced here: 81.1 us
  Pallas kernels  73.1 us (90%)
  local copies, waits for them, and re-layouts  6.02 us (7%)
  between operations  1.94 us (2%)
    pallas_call x1, Pallas kernels, fused_body(): pl.pallas_call(functools.partial(fused, dims), out_shape=(out(planes, ran...  73.1 us
    unnamed x8, local copies, waits for them, and re-layouts  5.34 us

profile of v3, /device:TPU:0, one launch (start us, length us, event | category | flops | bytes accessed | tf_op | source)
XLA Modules:
  0.0 81.1 jit_solution(17627065262503684067)
XLA Ops:
  1.9 0.0 copy-start
  1.9 2.2 %copy-done = f32[4,16,32,512]{3,2,1,0:T(8,128)S(1)} copy-done((f32[4,16,32,512]{3,2,1,0:T(8,128)S(1)}, f32[4,16,32,512]{3,2,1,0:T(8,128)}, u32[]{:S(2)}) %copy-start) | copy-done | bytes 4194328
  4.1 0.0 copy-start.1
  4.1 0.9 %copy-done.1 = f32[512,128]{1,0:T(8,128)S(1)} copy-done((f32[512,128]{1,0:T(8,128)S(1)}, f32[512,128]{1,0:T(8,128)}, u32[]{:S(2)}) %copy-start.1) | copy-done | bytes 262168
  5.1 0.0 copy-start.2
  5.1 0.7 copy-done.2
  5.8 73.1 %shard_map.76 = (f32[4,8,32,128]{3,2,1,0:T(8,128)S(1)}, f32[512,128]{1,0:T(8,128)S(1)}, f32[64,32]{1,0:T(8,128)S(1)}) custom-call(s32[1]{0:T(128)S(6)} %copy.11.rank_x, s32[1]{0:T(128)S(6)} %copy.12.rank_y, f32[2048,512]{1,0:T(8,128)S(1)} %bitcast.2, f32[512,128]{1,0:T(8,128)S(1)} %copy-done.1, f32[32,64]{1,0:T(8,128)S(1)} %bitcast.3), custom_call_target="tpu_custom_call" | custom-call | tf_op jit(solution)/shard_map/pallas_call | solution.py:284
  78.9 0.7 copy.8
  79.6 0.8 copy.13
  80.4 0.7 copy.14
Async XLA Ops:
  1.9 2.2 %copy-start = (f32[4,16,32,512]{3,2,1,0:T(8,128)S(1)}, f32[4,16,32,512]{3,2,1,0:T(8,128)}, u32[]{:S(2)}) copy-start(f32[4,16,32,512]{3,2,1,0:T(8,128)} %param.5) | copy-start | bytes 12582916
  4.1 0.9 %copy-start.1 = (f32[512,128]{1,0:T(8,128)S(1)}, f32[512,128]{1,0:T(8,128)}, u32[]{:S(2)}) copy-start(f32[512,128]{1,0:T(8,128)} %omega_x.1) | copy-start | bytes 786436
  5.1 0.7 copy-start.2

commit v4 on v3

--- a/solution.py
+++ b/solution.py
@@ -57,16 +57,16 @@
     return lax.dot_general(a, b, NT, precision=HIGHEST, preferred_element_type=jnp.float32)
 
 
-def split(x):
-    high = x.astype(jnp.bfloat16)
-    return high, (x - high.astype(jnp.float32)).astype(jnp.bfloat16)
-
-
-def mm3(a, b, dims=(((1,), (0,)), ((), ()))):
-    def one(x, y):
+def split(a):
+    high = a.astype(jnp.bfloat16)
+    return high, (a - high.astype(jnp.float32)).astype(jnp.bfloat16)
+
+
+def mm_split(a, b, dims=(((1,), (0,)), ((), ()))):
+    def dot(x, y):
         return lax.dot_general(x, y, dims, preferred_element_type=jnp.float32)
 
-    return one(a[0], b[0]) + (one(a[0], b[1]) + one(a[1], b[0]))
+    return dot(a[0], b[0]) + (dot(a[0], b[1]) + dot(a[1], b[0]))
 
 
 def eliminate(work, inv, size):
@@ -81,7 +81,7 @@
         row = work[pl.ds(j, 1), :]
         column = jnp.sum(jnp.where(cols == j, full, 0.0), axis=1, keepdims=True)
         pivot = jnp.sum(jnp.where(lane_ids == j, row, 0.0), axis=1, keepdims=True)
-        factor = jnp.where(row_ids > j, column / pivot, 0.0)
+        factor = jnp.where(row_ids > j, column * (1.0 / pivot), 0.0)
         inv_row = inv[pl.ds(j, 1), :]
         work[...] = full - factor * row
         inv[...] = inv[...] - factor * inv_row
@@ -125,8 +125,8 @@
 
     def sketch_step(c, carry):
         block = split(field[pl.ds(pl.multiple_of(c * chunk, chunk), chunk), :])
-        proj = mm3(block, omega)
-        part[...] += mm3(split(proj.T), block)
+        proj = mm_split(block, omega)
+        part[...] += mm_split(split(proj.T), block)
         return carry
 
     lax.fori_loop(0, planes * per_plane, sketch_step, 0)
@@ -176,7 +176,7 @@
     for v in range(planes):
         for c in range(per_plane):
             start = (v * per_plane + c) * chunk
-            tmp[pl.ds(c * chunk, chunk), :] = mm3(split(field[pl.ds(start, chunk), :]), sketch_parts, NT)
+            tmp[pl.ds(c * chunk, chunk), :] = mm_split(split(field[pl.ds(start, chunk), :]), sketch_parts, NT)
         for z in range(rows_z):
             terms[v, z] = tmp[pl.ds(z, rows_y, stride=rows_z), :]
         for y in others_y:

time: 81.4 us -> 81.4 us (level)
  no operation moved by 1% of the time
where the time goes in v4:
time: 81.4 us; the launch traced here: 81.1 us
  Pallas kernels  73.1 us (90%)
  local copies, waits for them, and re-layouts  6.02 us (7%)
  between operations  1.94 us (2%)
    pallas_call x1, Pallas kernels, fused_body(): pl.pallas_call(functools.partial(fused, dims), out_shape=(out(planes, ran...  73.1 us
    unnamed x8, local copies, waits for them, and re-layouts  5.34 us

profile of v4, /device:TPU:0, one launch (start us, length us, event | category | flops | bytes accessed | tf_op | source)
XLA Modules:
  0.0 81.1 jit_solution(9061144981861684139)
XLA Ops:
  1.9 0.0 copy-start
  1.9 2.2 %copy-done = f32[4,16,32,512]{3,2,1,0:T(8,128)S(1)} copy-done((f32[4,16,32,512]{3,2,1,0:T(8,128)S(1)}, f32[4,16,32,512]{3,2,1,0:T(8,128)}, u32[]{:S(2)}) %copy-start) | copy-done | bytes 4194328
  4.1 0.0 copy-start.1
  4.1 0.9 %copy-done.1 = f32[512,128]{1,0:T(8,128)S(1)} copy-done((f32[512,128]{1,0:T(8,128)S(1)}, f32[512,128]{1,0:T(8,128)}, u32[]{:S(2)}) %copy-start.1) | copy-done | bytes 262168
  5.1 0.0 copy-start.2
  5.1 0.7 copy-done.2
  5.8 73.1 %shard_map.76 = (f32[4,8,32,128]{3,2,1,0:T(8,128)S(1)}, f32[512,128]{1,0:T(8,128)S(1)}, f32[64,32]{1,0:T(8,128)S(1)}) custom-call(s32[1]{0:T(128)S(6)} %copy.11.rank_x, s32[1]{0:T(128)S(6)} %copy.12.rank_y, f32[2048,512]{1,0:T(8,128)S(1)} %bitcast.2, f32[512,128]{1,0:T(8,128)S(1)} %copy-done.1, f32[32,64]{1,0:T(8,128)S(1)} %bitcast.3), custom_call_target="tpu_custom_call" | custom-call | tf_op jit(solution)/shard_map/pallas_call | solution.py:284
  78.9 0.7 copy.8
  79.6 0.8 copy.13
  80.4 0.7 copy.14
Async XLA Ops:
  1.9 2.2 %copy-start = (f32[4,16,32,512]{3,2,1,0:T(8,128)S(1)}, f32[4,16,32,512]{3,2,1,0:T(8,128)}, u32[]{:S(2)}) copy-start(f32[4,16,32,512]{3,2,1,0:T(8,128)} %param.5) | copy-start | bytes 12582916
  4.1 0.9 %copy-start.1 = (f32[512,128]{1,0:T(8,128)S(1)}, f32[512,128]{1,0:T(8,128)}, u32[]{:S(2)}) copy-start(f32[512,128]{1,0:T(8,128)} %omega_x.1) | copy-start | bytes 786436
  5.1 0.7 copy-start.2
